TPU v7x, 32 devices: a whole 2x2x4 slice. The times are simulated.
32 devices in a mesh: parts: 2 (over x), blk: 16 (over z, y, core).
Axes of the slice: x: 2, y: 2, z: 4, core: 2. Of those that a mesh axis runs over, the one named last changes fastest.
Arguments:
- half_blocks: bfloat16 [4096, 24000], P(('parts', 'blk')), parts along dimension 0, may hold values from -6 to 6
Outputs:
- exchange_band: float32 [4096, 640], P(('parts', 'blk')), parts along dimension 0
There are 2 independent parts, one for each index of `parts`. A program takes and returns all parts, laid end to end along the dimension named above; each array names one. Nothing has to cross between parts.
All inputs are finite; a program needn't handle non-finite values.
Results may differ from a plain program's by a relative error of at most 0.0003.
Values may be sent and summed in bfloat16 or wider, within the bound.
A program may use at most 64 MiB of HBM per device.

v0:
```python
import math

import jax
import jax.numpy as jnp
from jax import lax
from jax.sharding import PartitionSpec as P


def from_behind(block, axis, distance):
    devices = range(lax.axis_size(axis))
    route = [((i - distance) % len(devices), i) for i in devices]
    return lax.ppermute(block, axis, route)


def make_tile(mine, other, factor):
    product = lax.dot_general(
        mine, other, (((1,), (1,)), ((), ())), preferred_element_type=jnp.float32
    )
    return product * factor


def body(half_blocks):
    depth = half_blocks.shape[1]
    factor = 1.0 / math.sqrt(depth)
    own_tile = make_tile(half_blocks, half_blocks, factor)
    current = half_blocks
    fetched = []
    for step in range(2):
        current = from_behind(current, "blk", 1)
        fetched.append(current)
    lower_one = fetched[0]
    lower_two = fetched[1]
    tile_minus_one = make_tile(half_blocks, lower_one, factor)
    tile_minus_two = make_tile(half_blocks, lower_two, factor)
    current = half_blocks
    upper = []
    for step in range(2):
        current = from_behind(current, "blk", -1)
        upper.append(current)
    tile_plus_one = make_tile(half_blocks, upper[0], factor)
    tile_plus_two = make_tile(half_blocks, upper[1], factor)
    return jnp.concatenate(
        [tile_minus_two, tile_minus_one, own_tile, tile_plus_one, tile_plus_two], axis=1
    )


def solution(mesh):
    return jax.shard_map(
        body,
        mesh=mesh,
        in_specs=(P(("parts", "blk"), None),),
        out_specs=P(("parts", "blk"), None),
        check_vma=False,
    )
```

profile of v0, /device:TPU:1, one launch (start us, length us, event | category | flops | bytes accessed | tf_op | source)
XLA Modules:
  0.0 284.3 jit_solution(3557586058681945132)
XLA Ops:
  0.0 0.0 copy-start
  0.0 2.6 collective-permute-start
  2.6 0.0 collective-permute-start.2
  2.6 132.5 %collective-permute-done = bf16[128,24000]{0,1:T(8,128)(2,1)S(1)} collective-permute-done((bf16[128,24000]{0,1:T(8,128)(2,1)}, bf16[128,24000]{0,1:T(8,128)(2,1)S(1)}, u32[]{:S(2)}, u32[]{:S(2)}) %collective-permute-start) | collective-permute-done | bytes 6144032 | tf_op jit(solution)/shard_map/ppermute | solution.py:12
  135.1 2.4 collective-permute-start.1
  137.5 65.8 %collective-permute-done.2 = bf16[128,24000]{0,1:T(8,128)(2,1)S(1)} collective-permute-done((bf16[128,24000]{0,1:T(8,128)(2,1)}, bf16[128,24000]{0,1:T(8,128)(2,1)S(1)}, u32[]{:S(2)}, u32[]{:S(2)}) %collective-permute-start.2) | collective-permute-done | bytes 6144032 | tf_op jit(solution)/shard_map/ppermute | solution.py:12
  203.3 0.0 collective-permute-start.3
  203.3 65.7 %collective-permute-done.1 = bf16[128,24000]{0,1:T(8,128)(2,1)} collective-permute-done((bf16[128,24000]{0,1:T(8,128)(2,1)S(1)}, bf16[128,24000]{0,1:T(8,128)(2,1)}, u32[]{:S(2)}, u32[]{:S(2)}) %collective-permute-start.1) | collective-permute-done | bytes 6144032 | tf_op jit(solution)/shard_map/ppermute | solution.py:12
  269.0 6.5 %fusion.4 = f32[128,640]{0,1:T(8,128)S(1)} fusion(bf16[128,24000]{0,1:T(8,128)(2,1)} %param.1, bf16[128,24000]{0,1:T(8,128)(2,1)} %collective-permute-done.1), kind=kOutput, calls=%fused_computation.9 | convolution fusion | flops 786448384 | bytes 12353536 | tf_op jit(solution)/shard_map/dot_general | solution.py:16
  275.5 0.0 copy-done
  275.5 2.0 fusion.3
  277.4 2.0 fusion.2
  279.4 2.0 fusion.1
  281.4 0.0 collective-permute-done.3
  281.4 2.0 fusion
  283.4 0.9 copy.2
Async XLA Ops:
  0.0 275.5 %copy-start = (bf16[128,24000]{0,1:T(8,128)(2,1)S(1)}, bf16[128,24000]{0,1:T(8,128)(2,1)}, u32[]{:S(2)}) copy-start(bf16[128,24000]{0,1:T(8,128)(2,1)} %param.1) | copy-start | bytes 18432004
  0.0 135.1 %collective-permute-start = (bf16[128,24000]{0,1:T(8,128)(2,1)}, bf16[128,24000]{0,1:T(8,128)(2,1)S(1)}, u32[]{:S(2)}, u32[]{:S(2)}) collective-permute-start(bf16[128,24000]{0,1:T(8,128)(2,1)} %param.1), channel_id=1, source_target_pairs={{15,0},{0,1},{1,2},{2,3},{3,4},{4,5},{5,6},{6,7},{7,8},{8,9},{9,10... | collective-permute-start | bytes 18432008 | tf_op jit(solution)/shard_map/ppermute | solution.py:12
  2.6 200.7 %collective-permute-start.2 = (bf16[128,24000]{0,1:T(8,128)(2,1)}, bf16[128,24000]{0,1:T(8,128)(2,1)S(1)}, u32[]{:S(2)}, u32[]{:S(2)}) collective-permute-start(bf16[128,24000]{0,1:T(8,128)(2,1)} %param.1), channel_id=1, source_target_pairs={{1,0},{2,1},{3,2},{4,3},{5,4},{6,5},{7,6},{8,7},{9,8},{10,9},{11,1... | collective-permute-start | bytes 18432008 | tf_op jit(solution)/shard_map/ppermute | solution.py:12
  135.1 133.9 %collective-permute-start.1 = (bf16[128,24000]{0,1:T(8,128)(2,1)S(1)}, bf16[128,24000]{0,1:T(8,128)(2,1)}, u32[]{:S(2)}, u32[]{:S(2)}) collective-permute-start(bf16[128,24000]{0,1:T(8,128)(2,1)S(1)} %collective-permute-done), channel_id=1, source_target_pairs={{15,0},{0,1},{1,2},{2,3},{3,4},{4,5},{5,6},{6,7},{7,8},{8,9},{9,10... | collective-permute-start | bytes 18432008 | tf_op jit(solution)/shard_map/ppermute | solution.py:12
  203.3 78.1 %collective-permute-start.3 = (bf16[128,24000]{0,1:T(8,128)(2,1)S(1)}, bf16[128,24000]{0,1:T(8,128)(2,1)S(1)}, u32[]{:S(2)}, u32[]{:S(2)}) collective-permute-start(bf16[128,24000]{0,1:T(8,128)(2,1)S(1)} %collective-permute-done.2), channel_id=1, source_target_pairs={{1,0},{2,1},{3,2},{4,3},{5,4},{6,5},{7,6},{8,7},{9,8},{10,9},{11,1... | collective-permute-start | bytes 18432008 | tf_op jit(solution)/shard_map/ppermute | solution.py:12
where the time goes:
time: 284 us
  waiting for transfers between devices  264 us (93%)
  matrix products  14.3 us (5%)
  starting transfers between devices  5.01 us (2%)
    ppermute x4, waiting for transfers between devices, from_behind(): return lax.ppermute(block, axis, route)  264 us
    dot_general x5, matrix products, make_tile(): lax.dot_general(mine, other, (((1,), (1,)), ((), ())), preferred_element_...  14.3 us
  transfers between devices with their start and end apart: 4, of which 3 were waited for; matrix products, arithmetic and copies ran while one was open for 4% of the time, Pallas kernels for 0%

commit v1 on v0

v1 whole, which is shorter than its diff:
```python
import functools
import math

import jax
import jax.numpy as jnp
from jax import lax
from jax.experimental import pallas as pl
from jax.experimental.pallas import tpu as pltpu
from jax.sharding import PartitionSpec as P

TILE = 128
PIECES = 15
F32 = jnp.float32


def gram(left, right):
    return lax.dot_general(left, right, (((0,), (0,)), ((), ())), preferred_element_type=F32)


def kernel(
    n, a_ref, out_ref, mine, cols, other, spare, acc, peer, ymsg, lohi, zout, cross, crossrecv, diag,
    load_sem, send_sem, y_sem, z_sem, sib_sem, tail_send, tail_recv,
):
    depth = a_ref.shape[0]
    quarter = depth // 4
    size = quarter // PIECES
    rows = n // 4
    me = lax.axis_index("blk")
    k = lax.rem(me, 2)
    y = lax.rem(me // 2, 2)
    r = me // 4
    to_row = lax.rem(r + 2 * y - 1 + rows, rows)
    from_row = lax.rem(r - 2 * y + 1 + rows, rows)

    def dev(row, half, core):
        return row * 4 + half * 2 + core

    sibling = dev(r, y, 1 - k)
    barrier = pltpu.get_barrier_semaphore()
    partners = [sibling]
    for core in range(2):
        partners += [dev(r, 1 - y, core), dev(to_row, y, core), dev(from_row, y, core)]
    for partner in partners:
        pl.semaphore_signal(barrier, inc=1, device_id={"blk": partner})

    def span(half, core, start, count):
        return pl.ds(pl.multiple_of((half * 2 + core) * quarter + start, 16), count)

    load_all = pltpu.make_async_copy(a_ref, mine, load_sem.at[0])
    load_all.start()
    load_part = pltpu.make_async_copy(
        a_ref.at[span(y, k, 0, quarter)], cols.at[2 * y + k], load_sem.at[1]
    )
    load_part.start()
    acc[...] = jnp.zeros_like(acc)
    peer[0, 3] = jnp.zeros((TILE, TILE), F32)
    peer[1, 0] = jnp.zeros((TILE, TILE), F32)
    cross[...] = jnp.zeros_like(cross)
    diag[...] = jnp.zeros_like(diag)
    pl.semaphore_wait(barrier, len(partners))

    def y_copy(core, c, count, slot, sem):
        start = pl.multiple_of(c * size, 16)
        return pltpu.make_async_remote_copy(
            src_ref=a_ref.at[span(1 - y, core, start, count)],
            dst_ref=other.at[slot, pl.ds(start, count)],
            send_sem=send_sem.at[core],
            recv_sem=sem,
            device_id={"blk": dev(r, 1 - y, core)},
        )

    def z_copy(core, c, count, slot, sem):
        start = pl.multiple_of(c * size, 16)
        return pltpu.make_async_remote_copy(
            src_ref=a_ref.at[span(y, core, start, count)],
            dst_ref=cols.at[2 * (1 - y) + slot, pl.ds(start, count)],
            send_sem=send_sem.at[2 + core],
            recv_sem=sem,
            device_id={"blk": dev(to_row, y, core)},
        )

    def send(c, carry):
        for core in range(2):
            z_copy(core, c, size, k, z_sem.at[k, c]).start()
            y_copy(core, c, size, k, y_sem.at[k, c]).start()
        return carry

    send(0, 0)
    sib_one = pltpu.make_async_remote_copy(
        src_ref=a_ref.at[span(y, 1 - k, 0, quarter)],
        dst_ref=cols.at[2 * y + k],
        send_sem=send_sem.at[4],
        recv_sem=sib_sem.at[0],
        device_id={"blk": sibling},
    )
    sib_one.start()
    sib_two = pltpu.make_async_remote_copy(
        src_ref=a_ref.at[span(1 - y, 1 - k, 0, quarter)],
        dst_ref=spare,
        send_sem=send_sem.at[5],
        recv_sem=sib_sem.at[1],
        device_id={"blk": sibling},
    )
    sib_two.start()
    lax.fori_loop(1, PIECES, send, 0)

    load_all.wait()
    load_part.wait()

    def diag_step(c, carry):
        part = mine[pl.ds(pl.multiple_of(c * size, 16), size), :]
        diag[...] += gram(part, part)
        return carry

    lax.fori_loop(0, 4 * PIECES, diag_step, 0)

    pltpu.make_async_remote_copy(
        src_ref=a_ref.at[span(y, 1 - k, 0, quarter)],
        dst_ref=cols.at[2 * y + 1 - k],
        send_sem=send_sem.at[4],
        recv_sem=sib_sem.at[0],
        device_id={"blk": sibling},
    ).wait_recv()
    sib_two.wait_recv()

    def cross_step(c, carry):
        start = pl.multiple_of(c * size, 16)
        cross[...] += gram(cols[2 * y + 1 - k, pl.ds(start, size), :], mine[span(y, k, start, size), :])
        cross[...] += gram(spare[pl.ds(start, size), :], mine[span(1 - y, k, start, size), :])
        return carry

    lax.fori_loop(0, PIECES, cross_step, 0)

    send_cross = pltpu.make_async_remote_copy(
        src_ref=cross,
        dst_ref=crossrecv,
        send_sem=tail_send.at[0],
        recv_sem=tail_recv.at[0],
        device_id={"blk": sibling},
    )
    send_cross.start()

    def main_step(c, carry):
        for core in range(2):
            z_copy(core, c, size, core, z_sem.at[core, c]).wait_recv()
            y_copy(core, c, size, core, y_sem.at[core, c]).wait_recv()
        part = pl.ds(pl.multiple_of(c * size, 16), size)
        left = jnp.concatenate([other[0, part, :], other[1, part, :]], axis=1)
        right = jnp.concatenate([cols[t, part, :] for t in range(4)], axis=1)
        product = gram(left, right)
        for u in range(2):
            for t in range(u, u + 3):
                acc[u, t] += product[u * TILE : (u + 1) * TILE, t * TILE : (t + 1) * TILE]
        return carry

    lax.fori_loop(0, PIECES, main_step, 0)

    swaps = []
    for u in range(2):
        swap = pltpu.make_async_remote_copy(
            src_ref=acc.at[u, pl.ds(u, 3)],
            dst_ref=peer.at[u, pl.ds(u, 3)],
            send_sem=tail_send.at[1 + u],
            recv_sem=tail_recv.at[1 + u],
            device_id={"blk": sibling},
        )
        swap.start()
        swaps.append(swap)
    for u in range(2):
        swaps[u].wait_recv()
        for t in range(u, u + 3):
            peer[u, t] += acc[u, t]
    send_y = pltpu.make_async_remote_copy(
        src_ref=peer.at[k, pl.ds(k, 3)],
        dst_ref=ymsg,
        send_sem=tail_send.at[3],
        recv_sem=tail_recv.at[3],
        device_id={"blk": dev(r, 1 - y, k)},
    )
    send_y.start()
    for u in range(2):
        zout[u] = peer[u, 2 * (1 - y) + k].T
    send_z = pltpu.make_async_remote_copy(
        src_ref=zout,
        dst_ref=lohi.at[y],
        send_sem=tail_send.at[4],
        recv_sem=tail_recv.at[4],
        device_id={"blk": dev(from_row, y, k)},
    )
    send_z.start()
    for u in range(2):
        lohi[1 - y, u] = peer[u, 2 * y + k].T
    send_cross.wait_recv()
    out_ref[:, 2 * TILE : 3 * TILE] = diag[...]
    near = cross[...].T + crossrecv[...]
    send_z.wait_recv()
    send_y.wait_recv()

    @pl.when(k == 0)
    def _():
        out_ref[:, 0:TILE] = ymsg[0] + lohi[0, 0]
        out_ref[:, TILE : 2 * TILE] = ymsg[1] + lohi[0, 1]
        out_ref[:, 3 * TILE : 4 * TILE] = near
        out_ref[:, 4 * TILE : 5 * TILE] = ymsg[2] + lohi[1, 0]

    @pl.when(k == 1)
    def _():
        out_ref[:, 0:TILE] = ymsg[0] + lohi[0, 1]
        out_ref[:, TILE : 2 * TILE] = near
        out_ref[:, 3 * TILE : 4 * TILE] = ymsg[1] + lohi[1, 0]
        out_ref[:, 4 * TILE : 5 * TILE] = ymsg[2] + lohi[1, 1]

    for core in range(2):
        for copy in (y_copy, z_copy):
            copy(core, 0, quarter, k, y_sem.at[k, 0]).wait_send()
    sib_one.wait_send()
    sib_two.wait_send()
    send_cross.wait_send()
    for swap in swaps:
        swap.wait_send()
    send_y.wait_send()
    send_z.wait_send()


def body(n, half_blocks):
    columns = half_blocks.T
    depth, tile = columns.shape
    quarter = depth // 4
    band = pl.pallas_call(
        functools.partial(kernel, n),
        out_shape=jax.ShapeDtypeStruct((tile, 5 * tile), F32),
        in_specs=[pl.BlockSpec(memory_space=pl.ANY)],
        out_specs=pl.BlockSpec(memory_space=pltpu.VMEM),
        scratch_shapes=[
            pltpu.VMEM((depth, tile), jnp.bfloat16),
            pltpu.VMEM((4, quarter, tile), jnp.bfloat16),
            pltpu.VMEM((2, quarter, tile), jnp.bfloat16),
            pltpu.VMEM((quarter, tile), jnp.bfloat16),
            pltpu.VMEM((2, 4, tile, tile), F32),
            pltpu.VMEM((2, 4, tile, tile), F32),
            pltpu.VMEM((3, tile, tile), F32),
            pltpu.VMEM((2, 2, tile, tile), F32),
            pltpu.VMEM((2, tile, tile), F32),
            pltpu.VMEM((tile, tile), F32),
            pltpu.VMEM((tile, tile), F32),
            pltpu.VMEM((tile, tile), F32),
            pltpu.SemaphoreType.DMA((2,)),
            pltpu.SemaphoreType.DMA((6,)),
            pltpu.SemaphoreType.DMA((2, PIECES)),
            pltpu.SemaphoreType.DMA((2, PIECES)),
            pltpu.SemaphoreType.DMA((2,)),
            pltpu.SemaphoreType.DMA((5,)),
            pltpu.SemaphoreType.DMA((5,)),
        ],
        compiler_params=pltpu.CompilerParams(
            collective_id=0, has_side_effects=True, vmem_limit_bytes=60 * 1024 * 1024
        ),
    )(columns)
    return band * (1.0 / math.sqrt(depth))


def solution(mesh):
    return jax.shard_map(
        functools.partial(body, mesh.shape["blk"]),
        mesh=mesh,
        in_specs=(P(("parts", "blk"), None),),
        out_specs=P(("parts", "blk"), None),
        check_vma=False,
    )
```

time: 284 us -> 83.7 us (0.29)
  the two profiles are of different devices: /device:TPU:1 before, /device:TPU:0 now
where the time goes in v1:
time: 83.7 us; the launch traced here: 83.5 us
  Pallas kernels  81.8 us (98%)
  other arithmetic  1.73 us (2%)
    pallas_call x1, Pallas kernels, body(): pl.pallas_call(functools.partial(kernel, n), out_shape=jax.ShapeDtypeStru...  81.8 us
    mul x1, other arithmetic, body(): return band * (1.0 / math.sqrt(depth))  1.73 us

profile of v1, /device:TPU:0, one launch (start us, length us, event | category | flops | bytes accessed | tf_op | source)
XLA Modules:
  0.0 83.5 jit_solution(10863294536159917744)
XLA Ops:
  0.0 81.8 %shard_map.17 = f32[128,640]{1,0:T(8,128)} custom-call(bf16[24000,128]{1,0:T(8,128)(2,1)} %bitcast.1), custom_call_target="tpu_custom_call" | custom-call | tf_op jit(solution)/shard_map/pallas_call | solution.py:229
  81.8 1.7 %broadcast_multiply_fusion = f32[128,640]{1,0:T(8,128)} fusion(f32[128,640]{1,0:T(8,128)} %shard_map.17), kind=kLoop, calls=%fused_computation | loop fusion | flops 81920 | bytes 655360 | tf_op jit(solution)/shard_map/mul | solution.py:259

commit v2 on v1

--- a/solution.py
+++ b/solution.py
@@ -10,6 +10,7 @@
 
 TILE = 128
 PIECES = 15
+LEAD = 3
 F32 = jnp.float32
 
 
@@ -79,11 +80,23 @@
             device_id={"blk": dev(to_row, y, core)},
         )
 
-    def send(c, carry):
-        for core in range(2):
-            z_copy(core, c, size, k, z_sem.at[k, c]).start()
-            y_copy(core, c, size, k, y_sem.at[k, c]).start()
-        return carry
+    def send(wave, c):
+        @pl.when(k == lax.rem(y + wave, 2))
+        def _():
+            for core in range(2):
+                z_copy(core, c, size, k, z_sem.at[k, c]).start()
+
+        @pl.when(k != lax.rem(y + wave, 2))
+        def _():
+            for core in range(2):
+                y_copy(core, c, size, k, y_sem.at[k, c]).start()
+
+    def send_wave(wave, first):
+        def step(c, carry):
+            send(wave, c)
+            return carry
+
+        lax.fori_loop(first, PIECES, step, 0)
 
     send(0, 0)
     sib_one = pltpu.make_async_remote_copy(
@@ -102,7 +115,7 @@
         device_id={"blk": sibling},
     )
     sib_two.start()
-    lax.fori_loop(1, PIECES, send, 0)
+    send_wave(0, 1)
 
     load_all.wait()
     load_part.wait()
@@ -140,36 +153,43 @@
     )
     send_cross.start()
 
-    def main_step(c, carry):
-        for core in range(2):
-            z_copy(core, c, size, core, z_sem.at[core, c]).wait_recv()
-            y_copy(core, c, size, core, y_sem.at[core, c]).wait_recv()
+    waves = (y, 1 - y)
+
+    def arrive(u, c):
+        z_copy(0, c, size, u, z_sem.at[u, c]).wait_recv()
+        y_copy(0, c, size, u, y_sem.at[u, c]).wait_recv()
+
+    def multiply(u, c):
         part = pl.ds(pl.multiple_of(c * size, 16), size)
-        left = jnp.concatenate([other[0, part, :], other[1, part, :]], axis=1)
-        right = jnp.concatenate([cols[t, part, :] for t in range(4)], axis=1)
-        product = gram(left, right)
-        for u in range(2):
-            for t in range(u, u + 3):
-                acc[u, t] += product[u * TILE : (u + 1) * TILE, t * TILE : (t + 1) * TILE]
-        return carry
-
-    lax.fori_loop(0, PIECES, main_step, 0)
-
-    swaps = []
-    for u in range(2):
-        swap = pltpu.make_async_remote_copy(
+        right = jnp.concatenate([cols[u + t, part, :] for t in range(3)], axis=1)
+        product = gram(other[u, part, :], right)
+        for t in range(3):
+            acc[u, u + t] += product[:, t * TILE : (t + 1) * TILE]
+
+    def steps(u, first, last):
+        def step(c, carry):
+            arrive(u, c)
+            multiply(u, c)
+            return carry
+
+        lax.fori_loop(first, last, step, 0)
+
+    def swap(wave):
+        u = waves[wave]
+        return pltpu.make_async_remote_copy(
             src_ref=acc.at[u, pl.ds(u, 3)],
             dst_ref=peer.at[u, pl.ds(u, 3)],
-            send_sem=tail_send.at[1 + u],
-            recv_sem=tail_recv.at[1 + u],
+            send_sem=tail_send.at[1 + wave],
+            recv_sem=tail_recv.at[1 + wave],
             device_id={"blk": sibling},
         )
-        swap.start()
-        swaps.append(swap)
-    for u in range(2):
-        swaps[u].wait_recv()
-        for t in range(u, u + 3):
-            peer[u, t] += acc[u, t]
+
+    def add_swapped(wave):
+        u = waves[wave]
+        swap(wave).wait_recv()
+        for t in range(3):
+            peer[u, u + t] += acc[u, u + t]
+
     send_y = pltpu.make_async_remote_copy(
         src_ref=peer.at[k, pl.ds(k, 3)],
         dst_ref=ymsg,
@@ -177,24 +197,87 @@
         recv_sem=tail_recv.at[3],
         device_id={"blk": dev(r, 1 - y, k)},
     )
-    send_y.start()
-    for u in range(2):
-        zout[u] = peer[u, 2 * (1 - y) + k].T
-    send_z = pltpu.make_async_remote_copy(
-        src_ref=zout,
-        dst_ref=lohi.at[y],
-        send_sem=tail_send.at[4],
-        recv_sem=tail_recv.at[4],
-        device_id={"blk": dev(from_row, y, k)},
-    )
-    send_z.start()
-    for u in range(2):
+
+    def send_z(wave):
+        return pltpu.make_async_remote_copy(
+            src_ref=zout.at[wave],
+            dst_ref=lohi.at[y, waves[wave]],
+            send_sem=tail_send.at[4 + wave],
+            recv_sem=tail_recv.at[4 + wave],
+            device_id={"blk": dev(from_row, y, k)},
+        )
+
+    def turn_z(wave):
+        zout[wave] = peer[waves[wave], 2 * (1 - y) + k].T
+
+    def turn_own(wave):
+        u = waves[wave]
         lohi[1 - y, u] = peer[u, 2 * y + k].T
+
+    steps(waves[0], 0, PIECES - LEAD)
+    send_wave(1, 0)
+    steps(waves[0], PIECES - LEAD, PIECES)
+    swap(0).start()
+    steps(waves[1], 0, PIECES - LEAD)
+    add_swapped(0)
+    turn_z(0)
+    turn_own(0)
+    steps(waves[1], PIECES - LEAD, PIECES - 1)
+    arrive(waves[1], PIECES - 1)
+
+    @pl.when(k == y)
+    def _():
+        send_y.start()
+
+    @pl.when(k == y)
+    def _():
+        send_z(0).start()
+
+    multiply(waves[1], PIECES - 1)
+    late = waves[1]
+
+    def swap_late(col, sem):
+        return pltpu.make_async_remote_copy(
+            src_ref=acc.at[late, col],
+            dst_ref=peer.at[late, col],
+            send_sem=tail_send.at[sem],
+            recv_sem=tail_recv.at[sem],
+            device_id={"blk": sibling},
+        )
+
+    far = 2 * (1 - y)
+    near_col = 2 * y + late
+    swap_late(far + 1 - k, 2).start()
+
+    @pl.when(k == y)
+    def _():
+        swap_late(far + k, 6).start()
+        swap_late(near_col, 7).start()
+
+    swap_late(far + k, 2).wait_recv()
+    peer[late, far + k] += acc[late, far + k]
+    turn_z(1)
+    send_z(1).start()
+
+    @pl.when(k != y)
+    def _():
+        swap_late(far + 1 - k, 6).wait_recv()
+        peer[late, far + 1 - k] += acc[late, far + 1 - k]
+        swap_late(near_col, 7).wait_recv()
+        peer[late, near_col] += acc[late, near_col]
+        send_y.start()
+        turn_own(1)
+
     send_cross.wait_recv()
     out_ref[:, 2 * TILE : 3 * TILE] = diag[...]
     near = cross[...].T + crossrecv[...]
-    send_z.wait_recv()
     send_y.wait_recv()
+
+    @pl.when(k == y)
+    def _():
+        send_z(0).wait_recv()
+
+    send_z(1).wait_recv()
 
     @pl.when(k == 0)
     def _():
@@ -216,10 +299,17 @@
     sib_one.wait_send()
     sib_two.wait_send()
     send_cross.wait_send()
-    for swap in swaps:
-        swap.wait_send()
+    swap(0).wait_send()
+    swap_late(far + 1 - k, 2).wait_send()
+
+    @pl.when(k == y)
+    def _():
+        swap_late(far + k, 6).wait_send()
+        swap_late(near_col, 7).wait_send()
+        send_z(0).wait_send()
+
     send_y.wait_send()
-    send_z.wait_send()
+    send_z(1).wait_send()
 
 
 def body(n, half_blocks):
@@ -249,11 +339,11 @@
             pltpu.SemaphoreType.DMA((2, PIECES)),
             pltpu.SemaphoreType.DMA((2, PIECES)),
             pltpu.SemaphoreType.DMA((2,)),
-            pltpu.SemaphoreType.DMA((5,)),
-            pltpu.SemaphoreType.DMA((5,)),
+            pltpu.SemaphoreType.DMA((8,)),
+            pltpu.SemaphoreType.DMA((8,)),
         ],
         compiler_params=pltpu.CompilerParams(
-            collective_id=0, has_side_effects=True, vmem_limit_bytes=60 * 1024 * 1024
+            collective_id=0, has_side_effects=True, vmem_limit_bytes=50 * 1024 * 1024
         ),
     )(columns)
     return band * (1.0 / math.sqrt(depth))

time: 83.7 us -> 81.4 us (0.973)
  Pallas kernels: 81.8 us -> 80.4 us
  other arithmetic: 1.73 us -> 0.75 us
    pallas_call x1, Pallas kernels: 81.8 us -> 80.4 us  [body(): pl.pallas_call(functools.partial(kernel, n), out_shape=jax.ShapeDtypeStru...]
    mul x1, other arithmetic: 1.73 us -> 0.75 us  [body(): return band * (1.0 / math.sqrt(depth))]
where the time goes in v2:
time: 81.4 us; the launch traced here: 81.2 us
  Pallas kernels  80.4 us (99%)
    pallas_call x1, Pallas kernels, body(): pl.pallas_call(functools.partial(kernel, n), out_shape=jax.ShapeDtypeStru...  80.4 us

profile of v2, /device:TPU:0, one launch (start us, length us, event | category | flops | bytes accessed | tf_op | source)
XLA Modules:
  0.0 81.2 jit_solution(11689326723492631673)
XLA Ops:
  0.0 80.4 %shard_map.17 = f32[128,640]{1,0:T(8,128)S(1)} custom-call(bf16[24000,128]{1,0:T(8,128)(2,1)} %bitcast.1), custom_call_target="tpu_custom_call" | custom-call | tf_op jit(solution)/shard_map/pallas_call | solution.py:319
  80.5 0.8 broadcast_multiply_fusion
